TPU v7x, 32 devices: a whole 2x2x4 slice. The times are simulated.
32 devices in a mesh: row: 4 (over y, core), col: 8 (over z, x).
Axes of the slice: x: 2, y: 2, z: 4, core: 2. Of those that a mesh axis runs over, the one named last changes fastest.
Arguments:
- points: float32 [16, 16384], P(None, ('row', 'col')), may hold values from -0.125 to 1.125
- lengthscale: float32 [16], replicated, may hold values from 2 to 6, as said below
- noise_var: float32 [128], replicated, may hold values from 0.2 to 2
- groups: int32 [32], replicated, may hold values from 0 to 63
- targets: float32 [16384, 128], P(('row', 'col')), may hold values from -162 to 162, as said below
Outputs:
- solution_field: float32 [16384, 128], P(('row', 'col'))
- residual: float32 [16384, 128], P(('row', 'col'))
Inputs may be any that keep to these rules, and one draw needn't show every extreme that they name: Observed targets, real-valued. `lengthscale`: length scales, positive.
All inputs are finite; a program needn't handle non-finite values.
Results may differ from a plain program's by a relative error of at most 0.029.
Values may be sent and summed in bfloat16 or wider, within the bound.
A program may use at most 64 MiB of HBM per device.

v0:
```python
import jax
import jax.numpy as jnp
from jax import lax
from jax.sharding import PartitionSpec as P

RHS = 128
TILE = 512
ITERS = 2


def kernel_tile(row_coords, col_coords):
    row_norms = jnp.sum(row_coords * row_coords, axis=0)
    col_norms = jnp.sum(col_coords * col_coords, axis=0)
    crossed = lax.dot_general(
        row_coords,
        col_coords,
        (((0,), (0,)), ((), ())),
        precision=lax.Precision.HIGHEST,
        preferred_element_type=jnp.float32,
    )
    squared = jnp.maximum(row_norms[:, None] + col_norms[None, :] - 2.0 * crossed, 0.0)
    radius = jnp.sqrt(squared)
    support = jnp.maximum(1.0 - radius, 0.0)
    return (support**11 * (11.0 * radius + 1.0)).astype(jnp.bfloat16)


def per_device(points, lengthscale, noise_var, groups, targets):
    n_row = lax.axis_size("row")
    n_col = lax.axis_size("col")
    own_blocks = targets.shape[0] // TILE
    row_blocks = own_blocks * n_col
    col_blocks = own_blocks * n_row
    scaled = points / lengthscale[:, None]
    row_coords = lax.all_gather(scaled.astype(jnp.bfloat16), "col", axis=1, tiled=True).astype(
        scaled.dtype
    )
    col_coords = lax.all_gather(scaled.astype(jnp.bfloat16), "row", axis=1, tiled=True).astype(
        scaled.dtype
    )
    row_place = lax.axis_index("row")
    col_place = lax.axis_index("col")
    row_groups = lax.dynamic_slice_in_dim(groups, row_place * row_blocks, row_blocks, 0)
    col_groups = lax.dynamic_index_in_dim(
        groups.reshape(n_row, n_col, own_blocks), col_place, 1, keepdims=False
    ).reshape(col_blocks)
    flat_mask = (row_groups[:, None] == col_groups[None, :]).reshape(row_blocks * col_blocks)
    tile_count = jnp.sum(flat_mask.astype(jnp.int32))
    tile_order = jnp.nonzero(flat_mask, size=row_blocks * col_blocks, fill_value=0)[0].astype(
        jnp.int32
    )

    def square_sums(vector):
        return lax.psum(jnp.sum(vector * vector, axis=0), ("row", "col"))

    solution_field = jnp.zeros_like(targets)
    residual = targets
    direction = targets
    norm_now = square_sums(residual)
    for iteration in range(ITERS):
        narrow = direction.astype(jnp.bfloat16)
        operator_source = lax.all_gather(narrow, "row", axis=0, tiled=True)
        source = operator_source
        initial = jnp.zeros((row_blocks * TILE, RHS), jnp.float32)

        def one_tile(position, summed):
            flat_index = tile_order[position]
            row_slot = flat_index // col_blocks
            col_slot = flat_index % col_blocks
            left = lax.dynamic_slice_in_dim(row_coords, row_slot * TILE, TILE, 1)
            right = lax.dynamic_slice_in_dim(col_coords, col_slot * TILE, TILE, 1)
            values = kernel_tile(left, right)
            block_vec = lax.dynamic_slice_in_dim(source, col_slot * TILE, TILE, 0)
            product = jnp.dot(values, block_vec, preferred_element_type=jnp.float32)
            current = lax.dynamic_slice_in_dim(summed, row_slot * TILE, TILE, 0)
            return lax.dynamic_update_slice_in_dim(summed, current + product, row_slot * TILE, 0)

        partial_value = lax.fori_loop(0, tile_count, one_tile, initial)
        outgoing = partial_value.astype(jnp.bfloat16).reshape(n_col, own_blocks * TILE, RHS)
        incoming = lax.all_to_all(outgoing, "col", split_axis=0, concat_axis=0, tiled=True)
        operator_product = jnp.sum(incoming, axis=0, dtype=jnp.float32)
        image = noise_var[None, :] * direction + operator_product
        curve = lax.psum(jnp.sum(direction * image, axis=0), ("row", "col"))
        step_size = norm_now / curve
        solution_field = solution_field + step_size[None, :] * direction
        residual = residual - step_size[None, :] * image
        if iteration + 1 < ITERS:
            norm_next = square_sums(residual)
            direction = residual + (norm_next / norm_now)[None, :] * direction
            norm_now = norm_next
    return (solution_field, residual)


def solution(mesh):
    placed = (P(None, ("row", "col")), P(), P(), P(), P(("row", "col"), None))
    return jax.shard_map(
        per_device,
        mesh=mesh,
        in_specs=placed,
        out_specs=(P(("row", "col"), None), P(("row", "col"), None)),
        check_vma=False,
    )
```

profile of v0, /device:TPU:0, one launch (start us, length us, event | category | flops | bytes accessed | tf_op | source)
XLA Modules:
  0.0 310.6 jit_solution(953452571910392687)
XLA Ops:
  0.6 0.7 reshape.98
  1.4 0.7 dynamic_slice.67
  2.3 0.7 fusion.28
  3.1 0.8 divide_convert_fusion
  3.9 6.2 %all_gather.13 = bf16[16,2048]{1,0:T(8,128)(2,1)S(1)} all-gather(bf16[16,512]{1,0:T(8,128)(2,1)S(1)} %divide_convert_fusion), channel_id=1, replica_groups=mesh['row'=4,'col'=8] {'row'}, dimensions={1}, use_global_device_ids=true | all-gather | bytes 81920 | tf_op jit(solution)/shard_map/all_gather | solution.py:37
  10.1 31.3 %all_gather.12 = bf16[16,4096]{1,0:T(8,128)(2,1)S(1)} all-gather(bf16[16,512]{1,0:T(8,128)(2,1)S(1)} %divide_convert_fusion), channel_id=1, replica_groups=mesh['row'=4,'col'=8] {'col'}, dimensions={1}, use_global_device_ids=true | all-gather | bytes 147456 | tf_op jit(solution)/shard_map/all_gather | solution.py:34
  41.7 0.8 scatter_custom_fusion
  42.8 1.0 convert_element_type.65
  43.7 7.2 %all_gather.14 = bf16[2048,128]{1,0:T(8,128)(2,1)S(1)} all-gather(bf16[512,128]{1,0:T(8,128)(2,1)S(1)} %convert_element_type.65), channel_id=1, replica_groups=mesh['row'=4,'col'=8] {'row'}, dimensions={0}, use_global_device_ids=true | all-gather | bytes 655360 | tf_op jit(solution)/shard_map/all_gather | solution.py:61
  50.9 0.7 compare_select_fusion.3
  51.7 13.1 %while.24 = (s32[]{:T(128)}, f32[4096,128]{1,0:T(8,128)S(1)}, s32[]{:T(128)}, s32[32]{0:T(128)S(1)}, f32[16,4096]{1,0:T(8,128)S(1)}, /*index=5*/f32[16,2048]{1,0...) while((s32[]{:T(128)}, f32[4096,128]{1,0:T(8,128)S(1)}, ...), condition=%wide.region_9.10_spmd, body=%wide.region_6.9_spmd.sunk | while | flops 121469984 | bytes 1843714 | solution.py:77
  52.4 0.7 dynamic_slice.105
  55.9 1.7 fusion.50
  58.6 0.7 dynamic_slice.105
  62.1 1.7 fusion.50
  63.8 0.3 fusion.51
  64.8 1.1 convert_element_type.66
  65.9 14.4 %all-to-all-start = ((bf16[8,512,128]{2,1,0:T(8,128)(2,1)}), bf16[8,512,128]{2,1,0:T(8,128)(2,1)S(1)}, u32[]{:S(2)}, u32[]{:S(2)}) async-start(bf16[8,512,128]{2,1,0:T(8,128)(2,1)} %bitcast.3), calls=%async_computation | async-start | bytes 2097152 | tf_op jit(solution)/shard_map/all_to_all | solution.py:79
  80.3 25.6 %all-to-all-done = bf16[8,512,128]{2,1,0:T(8,128)(2,1)S(1)} async-done(((bf16[8,512,128]{2,1,0:T(8,128)(2,1)}), bf16[8,512,128]{2,1,0:T(8,128)(2,1)S(1)}, u32[]{:S(2)}, u32[]{:S(2)}) %all-to-all-start) | async-done | bytes 1048608 | tf_op jit(solution)/shard_map/all_to_all | solution.py:79
  106.1 51.4 %all-reduce = (f32[128]{0:T(128)S(1)}, f32[128]{0:T(128)S(1)}) all-reduce(f32[128]{0:T(128)S(1)} %get-tuple-element.195, f32[128]{0:T(128)S(1)} %get-tuple-element.194), channel_id=1, replica_groups=mesh['row'=4,'col'=8] {'row','col'}, use_global_device_ids=true, to_apply=%region_1.2 | all-reduce | flops 256 | bytes 2048 | tf_op jit(solution)/shard_map/psum | solution.py:53
  157.6 42.1 %psum.30 = f32[128]{0:T(128)S(1)} all-reduce(f32[128]{0:T(128)S(1)} %multiply_reduce_fusion.5), channel_id=1, replica_groups=mesh['row'=4,'col'=8] {'row','col'}, use_global_device_ids=true, to_apply=%region_14.15 | all-reduce | flops 128 | bytes 1024 | tf_op jit(solution)/shard_map/psum | solution.py:53
  199.7 0.6 copy-done.2
  200.4 8.0 %all_gather.15 = bf16[2048,128]{1,0:T(8,128)(2,1)S(1)} all-gather(bf16[512,128]{1,0:T(8,128)(2,1)S(1)} %fusion.26), channel_id=1, replica_groups=mesh['row'=4,'col'=8] {'row'}, dimensions={0}, use_global_device_ids=true | all-gather | bytes 655360 | tf_op jit(solution)/shard_map/all_gather | solution.py:61
  208.4 11.8 %while.25 = (s32[]{:T(128)}, f32[4096,128]{1,0:T(8,128)S(1)}, s32[]{:T(128)}, s32[32]{0:T(128)S(1)}, f32[16,4096]{1,0:T(8,128)S(1)}, /*index=5*/f32[16,2048]{1,0...) while((s32[]{:T(128)}, f32[4096,128]{1,0:T(8,128)S(1)}, ...), condition=%wide.region_18.19_spmd, body=%wide.region_15.18_spmd.sunk | while | flops 121469984 | bytes 1843714 | solution.py:77
  209.1 0.6 dynamic_slice.111
  212.0 1.7 fusion.56
  213.7 0.3 fusion.57
  214.7 0.6 dynamic_slice.111
  217.6 1.7 fusion.56
  220.4 38.8 %all_to_all.10 = bf16[8,512,128]{2,1,0:T(8,128)(2,1)S(1)} all-to-all(bf16[8,512,128]{2,1,0:T(8,128)(2,1)S(1)} %bitcast.15), channel_id=1, replica_groups=mesh['row'=4,'col'=8] {'col'}, dimensions={0} | all-to-all | bytes 2097152 | tf_op jit(solution)/shard_map/all_to_all | solution.py:79
  259.4 50.2 %psum.31 = f32[128]{0:T(128)S(1)} all-reduce(f32[128]{0:T(128)S(1)} %multiply_reduce_fusion.4), channel_id=1, replica_groups=mesh['row'=4,'col'=8] {'row','col'}, use_global_device_ids=true, to_apply=%region_21.22 | all-reduce | flops 128 | bytes 1024 | tf_op jit(solution)/shard_map/psum | solution.py:82
  309.7 0.9 multiply_subtract_fusion
  (36 shorter events, 2.6 us)
Async XLA Ops:
  65.9 40.1 %copy-start = (f32[512,128]{1,0:T(8,128)S(1)}, f32[512,128]{1,0:T(8,128)}, u32[]{:S(2)}) copy-start(f32[512,128]{1,0:T(8,128)} %param.13) | copy-start | bytes 786436
  65.9 40.1 %copy-start.1 = (f32[128]{0:T(128)S(1)}, f32[128]{0:T(128)}, u32[]{:S(2)}) copy-start(f32[128]{0:T(128)} %param.11) | copy-start | bytes 1540
  65.9 40.0 %all-to-all-start = ((bf16[8,512,128]{2,1,0:T(8,128)(2,1)}), bf16[8,512,128]{2,1,0:T(8,128)(2,1)S(1)}, u32[]{:S(2)}, u32[]{:S(2)}) async-start(bf16[8,512,128]{2,1,0:T(8,128)(2,1)} %bitcast.3), calls=%async_computation | async-start | bytes 2097152 | tf_op jit(solution)/shard_map/all_to_all | solution.py:79
  199.7 0.6 copy-start.2
  220.4 89.3 %copy-start.3 = (f32[128]{0:T(128)S(1)}, f32[128]{0:T(128)}, u32[]{:S(2)}) copy-start(f32[128]{0:T(128)} %copy-done.2) | copy-start | bytes 1540
where the time goes:
time: 309 us; the launch traced here: 311 us
  blocking collectives  235 us (76%)
  waiting for transfers between devices  25.6 us (8%)
  starting transfers between devices  14.4 us (5%)
  loops' own time  14.2 us (5%)
  matrix products  8.11 us (3%)
  other arithmetic  7.25 us (2%)
  local copies, waits for them, and re-layouts  5.18 us (2%)
    psum x2, blocking collectives, square_sums(): return lax.psum(jnp.sum(vector * vector, axis=0), ('row', 'col'))  93.5 us
    psum x1, blocking collectives, per_device(): curve = lax.psum(jnp.sum(direction * image, axis=0), ('row', 'col'))  50.2 us
    all_to_all x1, blocking collectives, per_device(): lax.all_to_all(outgoing, 'col', split_axis=0, concat_axis=0, tiled=True)  38.8 us
    all_gather x1, blocking collectives, per_device(): lax.all_gather(scaled.astype(jnp.bfloat16), 'col', axis=1, tiled=True)  31.3 us
    all_to_all x1, waiting for transfers between devices, per_device(): lax.all_to_all(outgoing, 'col', split_axis=0, concat_axis=0, tiled=True)  25.6 us
    all_gather x2, blocking collectives, per_device(): operator_source = lax.all_gather(narrow, 'row', axis=0, tiled=True)  15.2 us
    all_to_all x1, starting transfers between devices, per_device(): lax.all_to_all(outgoing, 'col', split_axis=0, concat_axis=0, tiled=True)  14.4 us
    another operation x2, loops' own time, per_device(): partial_value = lax.fori_loop(0, tile_count, one_tile, initial)  14.2 us
  transfers between devices with their start and end apart: 1, of which 1 were waited for; matrix products, arithmetic and copies ran while one was open for 0% of the time, Pallas kernels for 0%

commit v1 on v0

--- a/solution.py
+++ b/solution.py
@@ -1,11 +1,210 @@
+import functools
+
 import jax
 import jax.numpy as jnp
 from jax import lax
+from jax.experimental import pallas as pl
+from jax.experimental.pallas import tpu as pltpu
 from jax.sharding import PartitionSpec as P
 
-RHS = 128
 TILE = 512
 ITERS = 2
+RHS = 128
+CHUNK = 128
+GATHER_LIMIT = 64
+VMEM_LIMIT = 48 * 1024 * 1024
+
+
+def split3(value):
+    first = value.astype(jnp.bfloat16).astype(jnp.float32)
+    rest = value - first
+    second = rest.astype(jnp.bfloat16).astype(jnp.float32)
+    return first, second, rest - second
+
+
+def lifted(coords, factor, norm_at, one_at):
+    wide = coords.astype(jnp.float32)
+    parts = split3(jnp.sum(wide * wide, axis=0, keepdims=True))
+    row = lax.broadcasted_iota(jnp.int32, wide.shape, 0)
+    tail = jnp.where((row >= one_at) & (row < one_at + 3), 1.0, 0.0)
+    for place, part in enumerate(parts):
+        tail = jnp.where(row == norm_at + place, part, tail)
+    return jnp.concatenate([wide * factor, tail], axis=0).astype(jnp.bfloat16)
+
+
+def wendland(squared):
+    safe = jnp.maximum(squared, 1e-30)
+    radius = safe * lax.rsqrt(safe)
+    support = jnp.maximum(1.0 - radius, 0.0)
+    second = support * support
+    third = second * support
+    fourth = second * second
+    eighth = fourth * fourth
+    return ((eighth * third) * (12.0 - 11.0 * support)).astype(jnp.bfloat16)
+
+
+def first_kernel(order, count, own, coords, source, field, tiles, image, narrow, sums,
+                 left, right, built, vectors, vec_sems, tile_sems):
+    total = count[0]
+
+    def vector_copy(slot):
+        return pltpu.make_async_copy(
+            source.at[order[slot]], vectors.at[slot], vec_sems.at[slot]
+        )
+
+    def tile_copy(slot):
+        return pltpu.make_async_copy(built.at[slot], tiles.at[slot], tile_sems.at[slot])
+
+    def begin(slot, carry):
+        vector_copy(slot).start()
+        return carry
+
+    lax.fori_loop(0, total, begin, 0)
+    left[...] = lifted(own[...], 1.0, 0, 3).T
+    image[...] = jnp.zeros_like(image)
+
+    def one_tile(slot, carry):
+        right[...] = lifted(coords[order[slot]], -2.0, 3, 0)
+        vector_copy(slot).wait()
+        for start in range(0, TILE, CHUNK):
+            rows = pl.ds(start, CHUNK)
+            squared = jnp.dot(left[rows, :], right[...], preferred_element_type=jnp.float32)
+            values = wendland(squared)
+            built[slot, rows, :] = values
+            image[rows, :] += jnp.dot(values, vectors[slot], preferred_element_type=jnp.float32)
+        tile_copy(slot).start()
+        return carry
+
+    lax.fori_loop(0, total, one_tile, 0)
+    narrow[...] = image[...].astype(jnp.bfloat16)
+    sums[0:1, :] = jnp.sum(field[...] * field[...], axis=0, keepdims=True)
+    sums[1:2, :] = jnp.sum(field[...] * image[...], axis=0, keepdims=True)
+
+    def finish(slot, carry):
+        tile_copy(slot).wait()
+        return carry
+
+    lax.fori_loop(0, total, finish, 0)
+
+
+def second_kernel(order, count, tiles, source, image, field, noise, norms, sums, after, curved,
+                  built, vectors, twice, vec_sems, tile_sems):
+    total = count[0]
+
+    def vector_copy(slot):
+        return pltpu.make_async_copy(
+            source.at[order[slot]], vectors.at[slot], vec_sems.at[slot]
+        )
+
+    def tile_copy(slot):
+        return pltpu.make_async_copy(tiles.at[slot], built.at[slot], tile_sems.at[slot])
+
+    def begin(slot, carry):
+        vector_copy(slot).start()
+        tile_copy(slot).start()
+        return carry
+
+    lax.fori_loop(0, total, begin, 0)
+    twice[...] = jnp.zeros_like(twice)
+
+    def one_tile(slot, carry):
+        vector_copy(slot).wait()
+        tile_copy(slot).wait()
+        twice[...] += jnp.dot(built[slot], vectors[slot], preferred_element_type=jnp.float32)
+        return carry
+
+    lax.fori_loop(0, total, one_tile, 0)
+    variance = noise[...]
+    squares = norms[0:1, :]
+    step = squares / (variance * squares + norms[1:2, :])
+    target = field[...]
+    product = image[...]
+    applied = variance * target + product
+    residual = target - step * applied
+    again = variance * residual + product - step * (variance * product + twice[...])
+    after[...] = residual
+    curved[...] = again
+    sums[0:1, :] = jnp.sum(residual * residual, axis=0, keepdims=True)
+    sums[1:2, :] = jnp.sum(residual * again, axis=0, keepdims=True)
+    sums[2:3, :] = jnp.sum(residual * applied + target * again, axis=0, keepdims=True)
+
+
+def gathered_plan(points, lengthscale, noise_var, groups, targets):
+    blocks = groups.shape[0]
+    dims = points.shape[0]
+    rhs = targets.shape[1]
+    axes = ("row", "col")
+    here = lax.axis_index(axes)
+    narrow_points = (points / lengthscale[:, None]).astype(jnp.bfloat16)
+    coords = lax.all_gather(narrow_points, axes, axis=0, tiled=False)
+    source = lax.all_gather(targets.astype(jnp.bfloat16), axes, axis=0, tiled=False)
+
+    same = groups == lax.dynamic_index_in_dim(groups, here, 0, keepdims=False)
+    count = jnp.sum(same.astype(jnp.int32)).reshape(1)
+    ids = jnp.arange(blocks, dtype=jnp.int32)
+    place = jnp.cumsum(same.astype(jnp.int32)) - 1
+    order = jnp.sum(
+        jnp.where(same[None, :] & (place[None, :] == ids[:, None]), ids[None, :], 0), axis=1
+    ).astype(jnp.int32)
+
+    vmem = pl.BlockSpec(memory_space=pltpu.VMEM)
+    smem = pl.BlockSpec(memory_space=pltpu.SMEM)
+    anywhere = pl.BlockSpec(memory_space=pl.ANY)
+    whole = jax.ShapeDtypeStruct((TILE, rhs), jnp.float32)
+    few = jax.ShapeDtypeStruct((8, rhs), jnp.float32)
+    tiles, image, narrow, sums = pl.pallas_call(
+        first_kernel,
+        out_shape=[
+            jax.ShapeDtypeStruct((blocks, TILE, TILE), jnp.bfloat16),
+            whole,
+            jax.ShapeDtypeStruct((TILE, rhs), jnp.bfloat16),
+            few,
+        ],
+        in_specs=[smem, smem, vmem, vmem, anywhere, vmem],
+        out_specs=[anywhere, vmem, vmem, vmem],
+        scratch_shapes=[
+            pltpu.VMEM((TILE, 2 * dims), jnp.bfloat16),
+            pltpu.VMEM((2 * dims, TILE), jnp.bfloat16),
+            pltpu.VMEM((blocks, TILE, TILE), jnp.bfloat16),
+            pltpu.VMEM((blocks, TILE, rhs), jnp.bfloat16),
+            pltpu.SemaphoreType.DMA((blocks,)),
+            pltpu.SemaphoreType.DMA((blocks,)),
+        ],
+        compiler_params=pltpu.CompilerParams(vmem_limit_bytes=VMEM_LIMIT),
+        name="first_product",
+    )(order, count, narrow_points, coords, source, targets)
+
+    source = lax.all_gather(narrow, axes, axis=0, tiled=False)
+    norms = lax.psum(sums, axes)
+    variance = noise_var[None, :]
+    sums, residual, again = pl.pallas_call(
+        second_kernel,
+        out_shape=[few, whole, whole],
+        in_specs=[smem, smem, anywhere, anywhere, vmem, vmem, vmem, vmem],
+        out_specs=[vmem, vmem, vmem],
+        scratch_shapes=[
+            pltpu.VMEM((blocks, TILE, TILE), jnp.bfloat16),
+            pltpu.VMEM((blocks, TILE, rhs), jnp.bfloat16),
+            pltpu.VMEM((TILE, rhs), jnp.float32),
+            pltpu.SemaphoreType.DMA((blocks,)),
+            pltpu.SemaphoreType.DMA((blocks,)),
+        ],
+        compiler_params=pltpu.CompilerParams(vmem_limit_bytes=VMEM_LIMIT),
+        name="second_product",
+    )(order, count, tiles, source, image, targets, variance, norms)
+
+    last = lax.psum(sums, axes)
+    squares = norms[0:1]
+    curve = variance * squares + norms[1:2]
+    step = squares / curve
+    ratio = last[0:1] / squares
+    second_curve = last[1:2] + ratio * (last[2:3] + ratio * curve)
+    second_step = last[0:1] / second_curve
+    direction = residual + ratio * targets
+    applied = variance * targets + image
+    solution_field = step * targets + second_step * direction
+    residual = residual - second_step * (again + ratio * applied)
+    return (solution_field, residual)
 
 
 def kernel_tile(row_coords, col_coords):
@@ -92,8 +291,14 @@
 
 def solution(mesh):
     placed = (P(None, ("row", "col")), P(), P(), P(), P(("row", "col"), None))
+
+    def plan(points, lengthscale, noise_var, groups, targets):
+        whole_field = groups.shape[0] <= GATHER_LIMIT and groups.shape[0] == mesh.size
+        run = gathered_plan if whole_field else per_device
+        return run(points, lengthscale, noise_var, groups, targets)
+
     return jax.shard_map(
-        per_device,
+        plan,
         mesh=mesh,
         in_specs=placed,
         out_specs=(P(("row", "col"), None), P(("row", "col"), None)),

time: 309 us -> 211 us (0.68)
  blocking collectives: 235 us -> 156 us
  starting transfers between devices: 14.4 us -> 0.08 us
  loops' own time: 14.2 us -> 0 us
  between operations: 0.75 us -> 14.1 us
  matrix products: 8.11 us -> 0 us
  Pallas kernels: 0 us -> 7.91 us
  waiting for transfers between devices: 25.6 us -> 20.3 us
    psum x3 -> x2, blocking collectives: 144 us -> 82.4 us  [the longest x1 42 us: gathered_plan(): norms = lax.psum(sums, axes)]
    all_to_all x1 -> x0, blocking collectives: 38.8 us -> none  [per_device(): lax.all_to_all(outgoing, 'col', split_axis=0, concat_axis=0, tiled=True)]
    all_to_all x1 -> x0, waiting for transfers between devices: 25.6 us -> none  [per_device(): lax.all_to_all(outgoing, 'col', split_axis=0, concat_axis=0, tiled=True)]
    all_gather x4 -> x1, blocking collectives: 52.7 us -> 73.8 us  [gathered_plan(): coords = lax.all_gather(narrow_points, axes, axis=0, tiled=False)]
    all_gather x0 -> x2, waiting for transfers between devices: none -> 20.2 us  [the longest x1 20.2 us: gathered_plan(): source = lax.all_gather(narrow, axes, axis=0, tiled=False)]
    all_to_all x1 -> x0, starting transfers between devices: 14.4 us -> none  [per_device(): lax.all_to_all(outgoing, 'col', split_axis=0, concat_axis=0, tiled=True)]
    another operation x2 -> x0, loops' own time: 14.2 us -> none  [per_device(): partial_value = lax.fori_loop(0, tile_count, one_tile, initial)]
    dot_general x8 -> x0, matrix products: 8.11 us -> none  [the longest x4 6.9 us: kernel_tile(): lax.dot_general(row_coords, col_coords, (((0,), (0,)), ((), ())), precisi...]
  transfers between devices with their start and end apart: 1 -> 2, of which waited for: 1 -> 1; matrix products, arithmetic and copies ran while one was open for 0% -> 2% of each run, Pallas kernels for 0% -> 0%
where the time goes in v1:
time: 211 us
  blocking collectives  156 us (74%)
  waiting for transfers between devices  20.3 us (10%)
  between operations  14.1 us (7%)
  Pallas kernels  7.91 us (4%)
  local copies, waits for them, and re-layouts  6.67 us (3%)
  other arithmetic  5.66 us (3%)
    all_gather x1, blocking collectives, gathered_plan(): coords = lax.all_gather(narrow_points, axes, axis=0, tiled=False)  73.8 us
    psum x1, blocking collectives, gathered_plan(): norms = lax.psum(sums, axes)  42 us
    psum x1, blocking collectives, gathered_plan(): last = lax.psum(sums, axes)  40.4 us
    all_gather x1, waiting for transfers between devices, gathered_plan(): source = lax.all_gather(narrow, axes, axis=0, tiled=False)  20.2 us
    unnamed x10, local copies, waits for them, and re-layouts  5.34 us
    pallas_call x1, Pallas kernels, gathered_plan(): pl.pallas_call(first_kernel, out_shape=[jax.ShapeDtypeStruct((blocks, TIL...  4.49 us
  transfers between devices with their start and end apart: 2, of which 1 were waited for; matrix products, arithmetic and copies ran while one was open for 2% of the time, Pallas kernels for 0%

profile of v1, /device:TPU:0, one launch (start us, length us, event | category | flops | bytes accessed | tf_op | source)
XLA Modules:
  0.0 210.8 jit_solution(3268830399098322585)
XLA Ops:
  7.2 0.0 copy-start.1
  7.2 0.0 copy-start.4
  7.2 0.0 all-gather.6.cloned.1.call-start
  7.2 1.7 convert_element_type.12
  8.9 0.0 all-gather.6.cloned.1.call-update
  8.9 0.0 all-gather.8.cloned.1.call-start
  9.0 1.2 dynamic_slice.4
  10.2 2.0 convert_reduce_fusion
  12.2 0.1 copy.9
  12.3 0.1 reduce-window.8
  12.3 0.1 add_reduce_fusion
  12.4 0.1 select_reduce_fusion.order
  12.6 0.8 divide_convert_fusion.own
  13.4 73.8 %all-gather = bf16[512,512]{1,0:T(8,128)(2,1)S(1)} all-gather(bf16[16,512]{1,0:T(8,128)(2,1)S(1)} %divide_convert_fusion.own), channel_id=2, replica_groups=mesh['row'=4,'col'=8] {'row','col'}, dimensions={0}, use_global_device_ids=true | all-gather | bytes 540672 | tf_op jit(solution)/shard_map/all_gather | solution.py:139
  87.2 0.0 all-gather.6.cloned.1.call-done
  87.2 0.0 copy-start
  87.2 0.9 copy-done
  88.2 0.0 copy-start.2
  88.2 2.2 %copy-done.2 = bf16[16384,128]{1,0:T(8,128)(2,1)S(1)} copy-done((bf16[16384,128]{1,0:T(8,128)(2,1)S(1)}, bf16[16384,128]{1,0:T(8,128)(2,1)}, u32[]{:S(2)}) %copy-start.2) | copy-done | bytes 4194328
  90.4 4.5 %first_product.1 = (bf16[32,512,512]{2,1,0:T(8,128)(2,1)}, f32[512,128]{1,0:T(8,128)S(1)}, bf16[512,128]{1,0:T(8,128)(2,1)}, f32[8,128]{1,0:T(8,128)S(1)}) custom-call(s32[32]{0:T(128)S(1)} %select_reduce_fusion.order, s32[1]{0:T(128)} %bitcast.2.count, bf16[16,512]{1,0:T(8,128)(2,1)S(1)} %divide_convert_fusion.own, bf16[32,16,512]{2,1,0:T(8,128)(2,1)S(1)} %bitcast.20, ...), custom_call_target="tpu_custom_call" | custom-call | tf_op jit(solution)/shard_map/first_product/pallas_call | solution.py:155
  94.9 0.0 all-gather.8.cloned.1.call-update
  94.9 42.0 %psum.14.norms = f32[8,128]{1,0:T(8,128)S(1)} all-reduce(f32[8,128]{1,0:T(8,128)S(1)} %get-tuple-element.9), channel_id=1, replica_groups=mesh['row'=4,'col'=8] {'row','col'}, use_global_device_ids=true, to_apply=%region_3.4 | all-reduce | flops 1024 | bytes 8192 | tf_op jit(solution)/shard_map/psum | solution.py:178
  136.9 20.2 %all-gather.8.cloned.1.call-done = bf16[16384,128]{1,0:T(8,128)(2,1)} async-done(((bf16[512,128]{1,0:T(8,128)(2,1)}), bf16[16384,128]{1,0:T(8,128)(2,1)}) %all-gather.8.cloned.1.call-update) | async-done | bytes 4194320 | tf_op jit(solution)/shard_map/all_gather | solution.py:177
  157.1 0.0 copy-done.1
  157.1 0.0 copy-done.4
  157.1 0.0 copy-start.3
  157.1 2.2 %copy-done.3 = bf16[16384,128]{1,0:T(8,128)(2,1)S(1)} copy-done((bf16[16384,128]{1,0:T(8,128)(2,1)S(1)}, bf16[16384,128]{1,0:T(8,128)(2,1)}, u32[]{:S(2)}) %copy-start.3) | copy-done | bytes 4194328
  159.3 3.4 %second_product.1 = (f32[8,128]{1,0:T(8,128)S(1)}, f32[512,128]{1,0:T(8,128)S(1)}, f32[512,128]{1,0:T(8,128)S(1)}) custom-call(s32[32]{0:T(128)S(1)} %select_reduce_fusion.order, s32[1]{0:T(128)} %bitcast.2.count, bf16[32,512,512]{2,1,0:T(8,128)(2,1)} %get-tuple-element.10.tiles, bf16[32,512,128]{2,1,0:T(8,128)(2,1)S(1)} %bitcast.19, ...), custom_call_target="tpu_custom_call" | custom-call | tf_op jit(solution)/shard_map/second_product/pallas_call | solution.py:180
  162.7 40.4 %psum.15 = f32[8,128]{1,0:T(8,128)S(1)} all-reduce(f32[8,128]{1,0:T(8,128)S(1)} %get-tuple-element.13), channel_id=1, replica_groups=mesh['row'=4,'col'=8] {'row','col'}, use_global_device_ids=true, to_apply=%region_4.5 | all-reduce | flops 1024 | bytes 8192 | tf_op jit(solution)/shard_map/psum | solution.py:196
  203.1 0.9 multiply_subtract_fusion
  (2 shorter events, 0.0 us)
Async XLA Ops:
  7.2 149.9 %copy-start.1 = (f32[512,128]{1,0:T(8,128)S(1)}, f32[512,128]{1,0:T(8,128)}, u32[]{:S(2)}) copy-start(f32[512,128]{1,0:T(8,128)} %field.3) | copy-start | bytes 786436
  7.2 149.9 %copy-start.4 = (f32[128]{0:T(128)S(1)}, f32[128]{0:T(128)}, u32[]{:S(2)}) copy-start(f32[128]{0:T(128)} %param.7) | copy-start | bytes 1540
  7.2 80.1 %all-gather.6.cloned.1.call-start = ((), (), s32[]{:S(2)}) async-start(), calls=%async_computation | async-start | bytes 4325376 | tf_op jit(solution)/shard_map/all_gather | solution.py:140
  8.9 148.2 %all-gather.8.cloned.1.call-start = ((), (), s32[]{:S(2)}) async-start(), calls=%async_computation.1 | async-start | bytes 4325376 | tf_op jit(solution)/shard_map/all_gather | solution.py:177
  87.2 1.0 copy-start
  88.2 2.2 %copy-start.2 = (bf16[16384,128]{1,0:T(8,128)(2,1)S(1)}, bf16[16384,128]{1,0:T(8,128)(2,1)}, u32[]{:S(2)}) copy-start(bf16[16384,128]{1,0:T(8,128)(2,1)} %all-gather.6.cloned.1.call-done) | copy-start | bytes 12582916
  157.1 2.2 %copy-start.3 = (bf16[16384,128]{1,0:T(8,128)(2,1)S(1)}, bf16[16384,128]{1,0:T(8,128)(2,1)}, u32[]{:S(2)}) copy-start(bf16[16384,128]{1,0:T(8,128)(2,1)} %all-gather.8.cloned.1.call-done) | copy-start | bytes 12582916
Sparse Core Ops, SparseCore 0:
  11.6 67.1 all-gather.5
  95.0 62.0 all-gather.7

commit v2 on v1

--- a/solution.py
+++ b/solution.py
@@ -1,3 +1,5 @@
+import functools
+
 import functools
 
 import jax
@@ -13,6 +15,7 @@
 CHUNK = 128
 GATHER_LIMIT = 64
 VMEM_LIMIT = 48 * 1024 * 1024
+MESH = pl.DeviceIdType.MESH
 
 
 def split3(value):
@@ -43,9 +46,177 @@
     return ((eighth * third) * (12.0 - 11.0 * support)).astype(jnp.bfloat16)
 
 
-def first_kernel(order, count, own, coords, source, field, tiles, image, narrow, sums,
-                 left, right, built, vectors, vec_sems, tile_sems):
-    total = count[0]
+def place():
+    row, col = lax.axis_index("row"), lax.axis_index("col")
+    return row // 2, lax.rem(row, 2), col // 2, lax.rem(col, 2)
+
+
+def greet(targets):
+    barrier = pltpu.get_barrier_semaphore()
+    for target in targets:
+        pl.semaphore_signal(barrier, inc=1, device_id=target, device_id_type=MESH)
+    pl.semaphore_wait(barrier, len(targets))
+
+
+def spread(n_col, cut, own, out, send_sems, recv_sems, own_sem):
+    y, core, z, x = place()
+    depth = n_col // 2
+    height = own.shape[0]
+    parts = (pl.ds(0, cut), pl.ds(cut, height - cut))
+
+    def device(y, core, z, x):
+        return (2 * y + core, 2 * z + x)
+
+    def number(y, core, z, x):
+        return (2 * y + core) * n_col + 2 * z + x
+
+    def level(step):
+        return lax.rem(z + step, depth)
+
+    over_x, over_y = device(y, core, z, 1 - x), device(1 - y, core, z, x)
+    over_core = device(y, 1 - core, z, x)
+    over_z = [device(y, core, level(depth - step), x) for step in range(1, depth)]
+    greet([over_x, over_y, over_core] + over_z)
+    started = []
+
+    def send(block, half, target, first=False):
+        spot = out.at[block, parts[half], :]
+        copy = pltpu.make_async_remote_copy(
+            src_ref=own.at[parts[half], :] if first else spot,
+            dst_ref=spot,
+            send_sem=send_sems.at[len(started)],
+            recv_sem=recv_sems.at[block, half],
+            device_id=target,
+            device_id_type=MESH,
+        )
+        copy.start()
+        started.append(copy)
+
+    def arrived(block, half):
+        spot = out.at[block, parts[half], :]
+        pltpu.make_async_copy(spot, spot, recv_sems.at[block, half]).wait()
+
+    def pass_on(block, first=False):
+        send(block, 0, over_x, first)
+        send(block, 1, over_y, first)
+        send(block, 0, over_y, first)
+        send(block, 1, over_x, first)
+        send(block, 0, over_core, first)
+        send(block, 1, over_core, first)
+
+    me = number(y, core, z, x)
+    for target in over_z:
+        send(me, 0, target, True)
+        send(me, 1, target, True)
+    pass_on(me, True)
+    keep = pltpu.make_async_copy(own, out.at[me], own_sem)
+    keep.start()
+    for step in range(depth + 2):
+        if 0 < step < depth:
+            block = number(y, core, level(step), x)
+            arrived(block, 0)
+            arrived(block, 1)
+            pass_on(block)
+        if 0 < step <= depth:
+            here = level(step - 1)
+            block = number(y, core, here, 1 - x)
+            arrived(block, 0)
+            send(block, 0, over_y)
+            send(block, 0, over_core)
+            block = number(1 - y, core, here, x)
+            arrived(block, 1)
+            send(block, 1, over_x)
+            send(block, 1, over_core)
+        if step >= 2:
+            here = level(step - 2)
+            for block, half in (
+                (number(1 - y, core, here, x), 0),
+                (number(y, core, here, 1 - x), 1),
+                (number(1 - y, core, here, 1 - x), 0),
+                (number(1 - y, core, here, 1 - x), 1),
+            ):
+                arrived(block, half)
+                send(block, half, over_core)
+    for step in range(depth):
+        for other_y in (y, 1 - y):
+            for other_x in (x, 1 - x):
+                block = number(other_y, 1 - core, level(step), other_x)
+                arrived(block, 0)
+                arrived(block, 1)
+    keep.wait()
+    for copy in started:
+        copy.wait_send()
+
+
+def first_gather(n_col, points, scale, targets, out, own, send_sems, recv_sems, own_sem):
+    scaled = (points[...] / scale[...]).astype(jnp.bfloat16)
+    own[0:TILE, :] = targets[...].astype(jnp.bfloat16)
+    dims, lanes = points.shape[0], targets.shape[1]
+    for part in range(TILE // lanes):
+        own[TILE + part * dims:TILE + (part + 1) * dims, :] = scaled[:, part * lanes:(part + 1) * lanes]
+    spread(n_col, own.shape[0] // 2, own, out, send_sems, recv_sems, own_sem)
+
+
+def second_gather(n_col, own, out, send_sems, recv_sems, own_sem):
+    spread(n_col, TILE // 2 + 16, own, out, send_sems, recv_sems, own_sem)
+
+
+def total_kernel(n_col, blocks, sums, total, land, send_sems, recv_sems):
+    me = lax.axis_index("row") * n_col + lax.axis_index("col")
+
+    def peer(offset):
+        other = lax.rem(me + offset, blocks)
+        return (other // n_col, lax.rem(other, n_col))
+
+    barrier = pltpu.get_barrier_semaphore()
+
+    def hello(offset, carry):
+        pl.semaphore_signal(barrier, inc=1, device_id=peer(offset), device_id_type=MESH)
+        return carry
+
+    lax.fori_loop(1, blocks, hello, 0)
+    pl.semaphore_wait(barrier, blocks - 1)
+
+    def copy(offset):
+        return pltpu.make_async_remote_copy(
+            src_ref=sums,
+            dst_ref=land.at[offset],
+            send_sem=send_sems.at[offset],
+            recv_sem=recv_sems.at[offset],
+            device_id=peer(offset),
+            device_id_type=MESH,
+        )
+
+    def begin(offset, carry):
+        copy(offset).start()
+        return carry
+
+    lax.fori_loop(1, blocks, begin, 0)
+    land[0] = sums[...]
+
+    def finish(offset, carry):
+        copy(offset).wait()
+        return carry
+
+    lax.fori_loop(1, blocks, finish, 0)
+    total[...] = jnp.sum(land[...], axis=0)
+
+
+def find_tiles(blocks, groups, order):
+    me = lax.axis_index("row") * lax.axis_size("col") + lax.axis_index("col")
+    mine = groups[me]
+
+    def look(block, count):
+        order[count] = block
+        return count + (groups[block] == mine).astype(jnp.int32)
+
+    return lax.fori_loop(0, blocks, look, 0)
+
+
+def first_kernel(blocks, groups, points, scale, field, source, tiles, image, narrow,
+                 order, left, right, built, vectors, vec_sems, tile_sems):
+    total = find_tiles(blocks, groups, order)
+    dims, lanes = points.shape[0], field.shape[1]
 
     def vector_copy(slot):
         return pltpu.make_async_copy(
@@ -60,25 +231,33 @@
         return carry
 
     lax.fori_loop(0, total, begin, 0)
-    left[...] = lifted(own[...], 1.0, 0, 3).T
+    left[...] = lifted((points[...] / scale[...]).astype(jnp.bfloat16), 1.0, 0, 3).T
     image[...] = jnp.zeros_like(image)
 
     def one_tile(slot, carry):
-        right[...] = lifted(coords[order[slot]], -2.0, 3, 0)
         vector_copy(slot).wait()
+        coords = jnp.concatenate(
+            [vectors[slot, pl.ds(TILE + part * dims, dims), :] for part in range(TILE // lanes)], axis=1
+        )
+        right[...] = lifted(coords, -2.0, 3, 0)
         for start in range(0, TILE, CHUNK):
             rows = pl.ds(start, CHUNK)
             squared = jnp.dot(left[rows, :], right[...], preferred_element_type=jnp.float32)
             values = wendland(squared)
             built[slot, rows, :] = values
-            image[rows, :] += jnp.dot(values, vectors[slot], preferred_element_type=jnp.float32)
+            image[rows, :] += jnp.dot(
+                values, vectors[slot, pl.ds(0, TILE), :], preferred_element_type=jnp.float32
+            )
         tile_copy(slot).start()
         return carry
 
     lax.fori_loop(0, total, one_tile, 0)
-    narrow[...] = image[...].astype(jnp.bfloat16)
-    sums[0:1, :] = jnp.sum(field[...] * field[...], axis=0, keepdims=True)
-    sums[1:2, :] = jnp.sum(field[...] * image[...], axis=0, keepdims=True)
+    narrow[0:TILE, :] = image[...].astype(jnp.bfloat16)
+    sums = split3(jnp.sum(field[...] * field[...], axis=0, keepdims=True)) + split3(
+        jnp.sum(field[...] * image[...], axis=0, keepdims=True)
+    )
+    zeros = jnp.zeros((16 - len(sums), lanes), jnp.float32)
+    narrow[TILE:TILE + 16, :] = jnp.concatenate(list(sums) + [zeros], axis=0).astype(jnp.bfloat16)
 
     def finish(slot, carry):
         tile_copy(slot).wait()
@@ -87,17 +266,20 @@
     lax.fori_loop(0, total, finish, 0)
 
 
-def second_kernel(order, count, tiles, source, image, field, noise, norms, sums, after, curved,
-                  built, vectors, twice, vec_sems, tile_sems):
-    total = count[0]
+def second_kernel(blocks, groups, tiles, source, image, field, noise, norms, sums, after, curved,
+                  order, built, vectors, twice, tails, vec_sems, tile_sems, tail_sem):
+    total = find_tiles(blocks, groups, order)
 
     def vector_copy(slot):
         return pltpu.make_async_copy(
-            source.at[order[slot]], vectors.at[slot], vec_sems.at[slot]
+            source.at[order[slot], pl.ds(0, TILE), :], vectors.at[slot], vec_sems.at[slot]
         )
 
     def tile_copy(slot):
         return pltpu.make_async_copy(tiles.at[slot], built.at[slot], tile_sems.at[slot])
+
+    tail_copy = pltpu.make_async_copy(source.at[:, pl.ds(TILE, 16), :], tails, tail_sem)
+    tail_copy.start()
 
     def begin(slot, carry):
         vector_copy(slot).start()
@@ -113,10 +295,15 @@
         twice[...] += jnp.dot(built[slot], vectors[slot], preferred_element_type=jnp.float32)
         return carry
 
+    tail_copy.wait()
     lax.fori_loop(0, total, one_tile, 0)
+    parts = jnp.sum(tails[...].astype(jnp.float32), axis=0)
     variance = noise[...]
-    squares = norms[0:1, :]
-    step = squares / (variance * squares + norms[1:2, :])
+    squares = parts[0:1, :] + parts[1:2, :] + parts[2:3, :]
+    curve = variance * squares + (parts[3:4, :] + parts[4:5, :] + parts[5:6, :])
+    norms[0:1, :] = squares
+    norms[1:2, :] = curve
+    step = squares / curve
     target = field[...]
     product = image[...]
     applied = variance * target + product
@@ -127,75 +314,112 @@
     sums[0:1, :] = jnp.sum(residual * residual, axis=0, keepdims=True)
     sums[1:2, :] = jnp.sum(residual * again, axis=0, keepdims=True)
     sums[2:3, :] = jnp.sum(residual * applied + target * again, axis=0, keepdims=True)
+    sums[3:8, :] = jnp.zeros((5, sums.shape[1]), jnp.float32)
 
 
 def gathered_plan(points, lengthscale, noise_var, groups, targets):
+    n_col = lax.axis_size("col")
     blocks = groups.shape[0]
     dims = points.shape[0]
     rhs = targets.shape[1]
-    axes = ("row", "col")
-    here = lax.axis_index(axes)
-    narrow_points = (points / lengthscale[:, None]).astype(jnp.bfloat16)
-    coords = lax.all_gather(narrow_points, axes, axis=0, tiled=False)
-    source = lax.all_gather(targets.astype(jnp.bfloat16), axes, axis=0, tiled=False)
-
-    same = groups == lax.dynamic_index_in_dim(groups, here, 0, keepdims=False)
-    count = jnp.sum(same.astype(jnp.int32)).reshape(1)
-    ids = jnp.arange(blocks, dtype=jnp.int32)
-    place = jnp.cumsum(same.astype(jnp.int32)) - 1
-    order = jnp.sum(
-        jnp.where(same[None, :] & (place[None, :] == ids[:, None]), ids[None, :], 0), axis=1
-    ).astype(jnp.int32)
+    scale = lengthscale[:, None]
+    variance = noise_var[None, :]
+    first_height = TILE + dims * TILE // rhs
+    second_height = TILE + 16
+    sends = 6 * (n_col // 2 - 1) * 2 + 6 + n_col // 2 * 8 - (n_col // 2 - 1) * 4
 
     vmem = pl.BlockSpec(memory_space=pltpu.VMEM)
     smem = pl.BlockSpec(memory_space=pltpu.SMEM)
     anywhere = pl.BlockSpec(memory_space=pl.ANY)
     whole = jax.ShapeDtypeStruct((TILE, rhs), jnp.float32)
     few = jax.ShapeDtypeStruct((8, rhs), jnp.float32)
-    tiles, image, narrow, sums = pl.pallas_call(
-        first_kernel,
+    gather_sems = [
+        pltpu.SemaphoreType.DMA((sends,)),
+        pltpu.SemaphoreType.DMA((blocks, 2)),
+        pltpu.SemaphoreType.DMA,
+    ]
+
+    def remote(number):
+        return pltpu.CompilerParams(
+            collective_id=number, has_side_effects=True, vmem_limit_bytes=VMEM_LIMIT
+        )
+
+    source = pl.pallas_call(
+        functools.partial(first_gather, n_col),
+        out_shape=jax.ShapeDtypeStruct((blocks, first_height, rhs), jnp.bfloat16),
+        in_specs=[vmem, vmem, vmem],
+        out_specs=anywhere,
+        scratch_shapes=[pltpu.VMEM((first_height, rhs), jnp.bfloat16)] + gather_sems,
+        compiler_params=remote(0),
+        name="first_gather",
+    )(points, scale, targets)
+
+    tiles, image, narrow = pl.pallas_call(
+        functools.partial(first_kernel, blocks),
         out_shape=[
             jax.ShapeDtypeStruct((blocks, TILE, TILE), jnp.bfloat16),
             whole,
-            jax.ShapeDtypeStruct((TILE, rhs), jnp.bfloat16),
-            few,
+            jax.ShapeDtypeStruct((second_height, rhs), jnp.bfloat16),
         ],
-        in_specs=[smem, smem, vmem, vmem, anywhere, vmem],
-        out_specs=[anywhere, vmem, vmem, vmem],
+        in_specs=[smem, vmem, vmem, vmem, anywhere],
+        out_specs=[anywhere, vmem, vmem],
         scratch_shapes=[
+            pltpu.SMEM((blocks,), jnp.int32),
             pltpu.VMEM((TILE, 2 * dims), jnp.bfloat16),
             pltpu.VMEM((2 * dims, TILE), jnp.bfloat16),
             pltpu.VMEM((blocks, TILE, TILE), jnp.bfloat16),
-            pltpu.VMEM((blocks, TILE, rhs), jnp.bfloat16),
+            pltpu.VMEM((blocks, first_height, rhs), jnp.bfloat16),
             pltpu.SemaphoreType.DMA((blocks,)),
             pltpu.SemaphoreType.DMA((blocks,)),
         ],
         compiler_params=pltpu.CompilerParams(vmem_limit_bytes=VMEM_LIMIT),
         name="first_product",
-    )(order, count, narrow_points, coords, source, targets)
-
-    source = lax.all_gather(narrow, axes, axis=0, tiled=False)
-    norms = lax.psum(sums, axes)
-    variance = noise_var[None, :]
-    sums, residual, again = pl.pallas_call(
-        second_kernel,
-        out_shape=[few, whole, whole],
-        in_specs=[smem, smem, anywhere, anywhere, vmem, vmem, vmem, vmem],
-        out_specs=[vmem, vmem, vmem],
+    )(groups, points, scale, targets, source)
+
+    source = pl.pallas_call(
+        functools.partial(second_gather, n_col),
+        out_shape=jax.ShapeDtypeStruct((blocks, second_height, rhs), jnp.bfloat16),
+        in_specs=[vmem],
+        out_specs=anywhere,
+        scratch_shapes=gather_sems,
+        compiler_params=remote(1),
+        name="second_gather",
+    )(narrow)
+
+    norms, sums, residual, again = pl.pallas_call(
+        functools.partial(second_kernel, blocks),
+        out_shape=[few, few, whole, whole],
+        in_specs=[smem, anywhere, anywhere, vmem, vmem, vmem],
+        out_specs=[vmem, vmem, vmem, vmem],
         scratch_shapes=[
+            pltpu.SMEM((blocks,), jnp.int32),
             pltpu.VMEM((blocks, TILE, TILE), jnp.bfloat16),
             pltpu.VMEM((blocks, TILE, rhs), jnp.bfloat16),
             pltpu.VMEM((TILE, rhs), jnp.float32),
+            pltpu.VMEM((blocks, 16, rhs), jnp.bfloat16),
+            pltpu.SemaphoreType.DMA((blocks,)),
+            pltpu.SemaphoreType.DMA((blocks,)),
+            pltpu.SemaphoreType.DMA,
+        ],
+        compiler_params=pltpu.CompilerParams(vmem_limit_bytes=VMEM_LIMIT),
+        name="second_product",
+    )(groups, tiles, source, image, targets, variance)
+
+    last = pl.pallas_call(
+        functools.partial(total_kernel, n_col, blocks),
+        out_shape=few,
+        in_specs=[vmem],
+        out_specs=vmem,
+        scratch_shapes=[
+            pltpu.VMEM((blocks, 8, rhs), jnp.float32),
             pltpu.SemaphoreType.DMA((blocks,)),
             pltpu.SemaphoreType.DMA((blocks,)),
         ],
-        compiler_params=pltpu.CompilerParams(vmem_limit_bytes=VMEM_LIMIT),
-        name="second_product",
-    )(order, count, tiles, source, image, targets, variance, norms)
-
-    last = lax.psum(sums, axes)
+        compiler_params=remote(2),
+        name="total",
+    )(sums)
     squares = norms[0:1]
-    curve = variance * squares + norms[1:2]
+    curve = norms[1:2]
     step = squares / curve
     ratio = last[0:1] / squares
     second_curve = last[1:2] + ratio * (last[2:3] + ratio * curve)
@@ -293,7 +517,9 @@
     placed = (P(None, ("row", "col")), P(), P(), P(), P(("row", "col"), None))
 
     def plan(points, lengthscale, noise_var, groups, targets):
-        whole_field = groups.shape[0] <= GATHER_LIMIT and groups.shape[0] == mesh.size
+        blocks = groups.shape[0]
+        square = mesh.shape["row"] == 4 and mesh.shape["col"] % 2 == 0
+        whole_field = blocks <= GATHER_LIMIT and blocks == mesh.size and square
         run = gathered_plan if whole_field else per_device
         return run(points, lengthscale, noise_var, groups, targets)
 

time: 211 us -> 85.9 us (0.41)
  blocking collectives: 156 us -> 0 us
  Pallas kernels: 7.91 us -> 81.4 us
  waiting for transfers between devices: 20.3 us -> 0 us
  between operations: 14.1 us -> 0.73 us
  other arithmetic: 5.66 us -> 0.91 us
  local copies, waits for them, and re-layouts: 6.67 us -> 2.46 us
    psum x2 -> x0, blocking collectives: 82.4 us -> none  [the longest x1 42 us: gathered_plan(): norms = lax.psum(sums, axes)]
    all_gather x1 -> x0, blocking collectives: 73.8 us -> none  [gathered_plan(): coords = lax.all_gather(narrow_points, axes, axis=0, tiled=False)]
    pallas_call x2 -> x5, Pallas kernels: 7.91 us -> 81.4 us  [the longest x1 34.1 us: gathered_plan(): pl.pallas_call(functools.partial(first_gather, n_col), out_shape=jax.Shap...]
    all_gather x2 -> x0, waiting for transfers between devices: 20.2 us -> none  [the longest x1 20.2 us: gathered_plan(): source = lax.all_gather(narrow, axes, axis=0, tiled=False)]
    unnamed x10, local copies, waits for them, and re-layouts: 5.34 us -> 1.72 us
    convert_element_type x2 -> x0, other arithmetic: 2.5 us -> none  [the longest x1 1.65 us: gathered_plan(): targets.astype(jnp.bfloat16)]
  transfers between devices with their start and end apart: 2 -> 0, of which waited for: 1 -> 0; matrix products, arithmetic and copies ran while one was open for 2% -> 0% of each run, Pallas kernels for 0% -> 0%
where the time goes in v2:
time: 85.9 us; the launch traced here: 85.5 us
  Pallas kernels  81.4 us (95%)
  local copies, waits for them, and re-layouts  2.46 us (3%)
  other arithmetic  0.91 us (1%)
    pallas_call x1, Pallas kernels, gathered_plan(): pl.pallas_call(functools.partial(first_gather, n_col), out_shape=jax.Shap...  34.1 us
    pallas_call x1, Pallas kernels, gathered_plan(): pl.pallas_call(functools.partial(second_gather, n_col), out_shape=jax.Sha...  31.4 us
    pallas_call x1, Pallas kernels, gathered_plan(): pl.pallas_call(functools.partial(total_kernel, n_col, blocks), out_shape=...  9.16 us
    pallas_call x1, Pallas kernels, gathered_plan(): pl.pallas_call(functools.partial(first_kernel, blocks), out_shape=[jax.Sh...  3.6 us
    pallas_call x1, Pallas kernels, gathered_plan(): pl.pallas_call(functools.partial(second_kernel, blocks), out_shape=[few,...  3.08 us
    unnamed x10, local copies, waits for them, and re-layouts  1.72 us

profile of v2, /device:TPU:0, one launch (start us, length us, event | category | flops | bytes accessed | tf_op | source)
XLA Modules:
  0.0 85.5 jit_solution(528315275300284894)
XLA Ops:
  0.6 0.0 copy-start.4
  0.6 0.7 copy.8.scale
  1.4 0.0 copy-start
  1.4 0.9 %copy-done = f32[512,128]{1,0:T(8,128)S(1)} copy-done((f32[512,128]{1,0:T(8,128)S(1)}, f32[512,128]{1,0:T(8,128)}, u32[]{:S(2)}) %copy-start) | copy-done | bytes 262168
  2.3 0.0 copy-start.2
  2.3 0.8 copy-done.2
  3.1 34.1 %first_gather.1.source = bf16[32,576,128]{2,1,0:T(8,128)(2,1)S(1)} custom-call(f32[16,512]{1,0:T(8,128)S(1)} %copy-done.2, f32[16,1]{1,0:T(8,128)S(1)} %copy.8.scale, f32[512,128]{1,0:T(8,128)S(1)} %copy-done), custom_call_target="tpu_custom_call" | custom-call | tf_op jit(solution)/shard_map/first_gather/pallas_call | solution.py:347
  37.2 0.0 copy-done.4
  37.2 0.0 copy-start.1
  37.3 0.0 copy-start.3
  37.3 3.6 %first_product.1 = (bf16[32,512,512]{2,1,0:T(8,128)(2,1)}, f32[512,128]{1,0:T(8,128)S(1)}, bf16[528,128]{1,0:T(8,128)(2,1)S(1)}) custom-call(s32[32]{0:T(128)S(1)} %copy-done.4, f32[16,512]{1,0:T(8,128)S(1)} %copy-done.2, f32[16,1]{1,0:T(8,128)S(1)} %copy.8.scale, f32[512,128]{1,0:T(8,128)S(1)} %copy-done, bf16[32,576,128]{2,1,0:T(8,128)(2,1)S(1)} %first_gather.1.source), custom_call_target="tpu_custom_call" | custom-call | tf_op jit(solution)/shard_map/first_product/pallas_call | solution.py:357
  40.9 31.4 %second_gather.1.source = bf16[32,528,128]{2,1,0:T(8,128)(2,1)S(1)} custom-call(bf16[528,128]{1,0:T(8,128)(2,1)S(1)} %get-tuple-element.10.own), custom_call_target="tpu_custom_call" | custom-call | tf_op jit(solution)/shard_map/second_gather/pallas_call | solution.py:379
  72.3 0.0 copy-done.1
  72.3 0.0 copy-done.3
  72.3 3.1 %second_product.1 = (f32[8,128]{1,0:T(8,128)S(1)}, f32[8,128]{1,0:T(8,128)S(1)}, f32[512,128]{1,0:T(8,128)S(1)}, f32[512,128]{1,0:T(8,128)S(1)}) custom-call(s32[32]{0:T(128)S(1)} %copy-done.4, bf16[32,512,512]{2,1,0:T(8,128)(2,1)} %get-tuple-element.9.tiles, bf16[32,528,128]{2,1,0:T(8,128)(2,1)S(1)} %second_gather.1.source, ...), custom_call_target="tpu_custom_call" | custom-call | tf_op jit(solution)/shard_map/second_product/pallas_call | solution.py:389
  75.4 9.2 %total.1 = f32[8,128]{1,0:T(8,128)S(1)} custom-call(f32[8,128]{1,0:T(8,128)S(1)} %get-tuple-element.13.sums), custom_call_target="tpu_custom_call" | custom-call | tf_op jit(solution)/shard_map/total/pallas_call | solution.py:408
  84.6 0.9 %multiply_subtract_fusion = (f32[512,128]{1,0:T(8,128)}, f32[512,128]{1,0:T(8,128)}) fusion(f32[512,128]{1,0:T(8,128)S(1)} %get-tuple-element.14, f32[512,128]{1,0:T(8,128)S(1)} %get-tuple-element.15, f32[512,128]{1,0:T(8,128)S(1)} %get-tuple-element.11.image, f32[512,128]{1,0:T(8,128)S(1)} %copy-done.1, f32[128]{0:T(128)S(1)} %copy-done.3, f32[128]{0:T(128)S(1)} %bitcast.8, ...), kind=kLoop, calls=%fused_computation | loop fusion | flops 720896 | bytes 1574912 | tf_op jit(solution)/shard_map/sub | solution.py:430
  (1 shorter events, 0.0 us)
Async XLA Ops:
  0.6 36.6 %copy-start.4 = (s32[32]{0:T(128)S(1)}, s32[32]{0:T(128)}, u32[]{:S(2)}) copy-start(s32[32]{0:T(128)} %groups.3) | copy-start | bytes 388
  1.4 0.9 %copy-start = (f32[512,128]{1,0:T(8,128)S(1)}, f32[512,128]{1,0:T(8,128)}, u32[]{:S(2)}) copy-start(f32[512,128]{1,0:T(8,128)} %field.3) | copy-start | bytes 786436
  2.3 0.8 copy-start.2
  37.2 35.1 %copy-start.1 = (f32[512,128]{1,0:T(8,128)S(1)}, f32[512,128]{1,0:T(8,128)}, u32[]{:S(2)}) copy-start(f32[512,128]{1,0:T(8,128)} %field.3) | copy-start | bytes 786436
  37.3 35.1 %copy-start.3 = (f32[128]{0:T(128)S(1)}, f32[128]{0:T(128)}, u32[]{:S(2)}) copy-start(f32[128]{0:T(128)} %param.7) | copy-start | bytes 1540
